TPU v7x, 32 devices: a whole 2x2x4 slice. The times are simulated.
32 devices in a mesh: row: 8 (over z, core), col: 4 (over y, x).
Axes of the slice: x: 2, y: 2, z: 4, core: 2. Of those that a mesh axis runs over, the one named last changes fastest.
Arguments:
- slab_block: bfloat16 [16384, 2048], P('row', 'col'), may hold values from -6 to 6
- scale_first: bfloat16 [16384], P('row'), may hold values from 0.5 to 2
- scale_second: bfloat16 [16384], P('row'), may hold values from 0.5 to 2
- panel_lower: bfloat16 [16384, 4096], P('row', 'col'), may hold values from -0.09375 to 0.09375
Outputs:
- updated_slab: bfloat16 [16384, 2048], P('row', 'col')
All inputs are finite; a program needn't handle non-finite values.
Results may differ from a plain program's by a relative error of at most 0.015.
Values may be sent and summed in bfloat16 or wider, within the bound.
A program may use at most 64 MiB of HBM per device.

v0:
```python
import jax
import jax.numpy as jnp
from jax import lax
from jax.sharding import PartitionSpec as P

PANEL_W = 4096


inv_root = 0.7071067811865476


def from_partner(block, axis, bit):
    count = lax.axis_size(axis)
    route = []
    for low in range(count):
        high = low | 1 << bit
        if high != low and high < count:
            route += [(low, high), (high, low)]
    return lax.ppermute(block, axis, route)


def per_device(slab_block, scale_first, scale_second, panel_lower):
    row_count, col_width = slab_block.shape
    groups = lax.axis_size("row")
    top_bit = groups.bit_length() - 1
    first = (scale_first.astype(jnp.float32)[:, None] * slab_block.astype(jnp.float32)).astype(
        jnp.bfloat16
    )
    my_index = lax.axis_index("row")
    partner = from_partner(first, "row", top_bit - 1)
    upper_one = my_index // (groups // 2) % 2 == 0
    own_vals = first.astype(jnp.float32)
    far_vals = partner.astype(jnp.float32)
    level_one = jnp.where(
        upper_one, (own_vals + far_vals) * inv_root, (far_vals - own_vals) * inv_root
    )
    second = (scale_second.astype(jnp.float32)[:, None] * level_one).astype(jnp.bfloat16)
    partner_two = from_partner(second, "row", top_bit - 2)
    upper_two = my_index // (groups // 4) % 2 == 0
    own_two = second.astype(jnp.float32)
    far_two = partner_two.astype(jnp.float32)
    level_two = jnp.where(upper_two, (own_two + far_two) * inv_root, (far_two - own_two) * inv_root)
    transformed = level_two.astype(jnp.bfloat16)
    moved = lax.all_to_all(
        transformed.reshape(row_count // groups, groups, col_width),
        "row",
        split_axis=1,
        concat_axis=0,
        tiled=True,
    )
    stored = moved.reshape(row_count, col_width)
    top_count = PANEL_W // groups
    top_local = stored[:top_count].reshape(top_count, 1, col_width)
    upper_rows = lax.all_gather(top_local, "row", axis=1, tiled=True).reshape(PANEL_W, col_width)
    block_width = panel_lower.shape[1]
    empty_sum = jnp.zeros((row_count, col_width), jnp.float32)
    shard_piece = lax.all_gather(panel_lower, "col", axis=1, tiled=True)
    blocks_in = shard_piece.shape[1] // block_width

    def one_block(blocknum, running):
        panel_part = lax.dynamic_slice_in_dim(shard_piece, blocknum * block_width, block_width, 1)
        rows_used = lax.dynamic_slice_in_dim(upper_rows, blocknum * block_width, block_width, 0)
        product = jnp.dot(panel_part, rows_used, preferred_element_type=jnp.float32)
        return running + product.astype(jnp.bfloat16).astype(jnp.float32)

    update_sum = lax.fori_loop(0, blocks_in, one_block, empty_sum)
    return (stored.astype(jnp.float32) - update_sum).astype(jnp.bfloat16)


def solution(mesh):
    placed = (P("row", "col"), P("row"), P("row"), P("row", "col"))
    return jax.shard_map(
        per_device, mesh=mesh, in_specs=placed, out_specs=P("row", "col"), check_vma=False
    )
```

profile of v0, /device:TPU:0, one launch (start us, length us, event | category | flops | bytes accessed | tf_op | source)
XLA Modules:
  0.0 459.1 jit_solution(17123206110217531893)
XLA Ops:
  6.5 0.0 copy-start
  6.5 0.0 all-gather.5.cloned.1.call-start
  6.5 0.7 convert_element_type.54
  7.2 2.0 multiply_convert_fusion
  9.3 4.1 collective-permute-start
  13.4 0.0 copy-done
  13.4 90.7 %collective-permute-done = bf16[2048,512]{1,0:T(8,128)(2,1)} collective-permute-done((bf16[2048,512]{1,0:T(8,128)(2,1)S(1)}, bf16[2048,512]{1,0:T(8,128)(2,1)}, u32[]{:S(2)}, u32[]{:S(2)}) %collective-permute-start) | collective-permute-done | bytes 2097184 | tf_op jit(solution)/shard_map/ppermute | solution.py:19
  104.1 3.0 fusion.12
  107.1 0.7 collective-permute-start.1
  107.8 46.3 %collective-permute-done.1 = bf16[2048,512]{1,0:T(8,128)(2,1)} collective-permute-done((bf16[2048,512]{1,0:T(8,128)(2,1)S(1)}, bf16[2048,512]{1,0:T(8,128)(2,1)}, u32[]{:S(2)}, u32[]{:S(2)}) %collective-permute-start.1) | collective-permute-done | bytes 2097184 | tf_op jit(solution)/shard_map/ppermute | solution.py:19
  154.1 2.7 fusion.19
  156.8 0.7 copy.8
  157.4 54.4 %all_to_all.15 = bf16[256,8,512]{2,0,1:T(8,128)(2,1)S(1)} all-to-all(bf16[256,8,512]{2,0,1:T(8,128)(2,1)S(1)} %copy.8), channel_id=1, replica_groups=mesh['row'=8,'col'=4] {'row'}, dimensions={1} | all-to-all | bytes 4194304 | tf_op jit(solution)/shard_map/all_to_all | solution.py:44
  211.8 0.8 slice.5
  212.7 0.0 all-gather.5.cloned.1.call-update
  212.7 0.0 all-gather.3.cloned.1.call-start
  212.8 0.7 all-gather.3.cloned.1.call-update
  213.5 45.5 %all-gather.5.cloned.1.call-done = bf16[512,8,512]{2,0,1:T(8,128)(2,1)} async-done(((bf16[512,1,512]{2,0,1:T(8,128)(2,1)}), bf16[512,8,512]{2,0,1:T(8,128)(2,1)}) %all-gather.5.cloned.1.call-update) | async-done | bytes 4194320 | tf_op jit(solution)/shard_map/all_gather | solution.py:54
  258.9 6.5 %copy.11 = bf16[512,8,512]{2,1,0:T(8,128)(2,1)} copy(bf16[512,8,512]{2,0,1:T(8,128)(2,1)} %all-gather.5.cloned.1.call-done) | data formatting | bytes 8388608 | tf_op jit(solution)/shard_map/all_gather | solution.py:54
  265.4 151.5 %all-gather.3.cloned.1.call-done = bf16[2048,4096]{1,0:T(8,128)(2,1)} async-done(((bf16[2048,1024]{1,0:T(8,128)(2,1)}), bf16[2048,4096]{1,0:T(8,128)(2,1)}) %all-gather.3.cloned.1.call-update) | async-done | bytes 16777232 | tf_op jit(solution)/shard_map/all_gather | solution.py:57
  416.9 31.2 %while.14 = (s32[]{:T(128)}, f32[2048,512]{1,0:T(8,128)}, bf16[2048,4096]{1,0:T(8,128)(2,1)}, bf16[4096,512]{1,0:T(8,128)(2,1)}, s32[]{:T(128)}, /*index=5*/s32[]{:T(128)}, s32[]{:T(128)}, s32[]{:T(128)}) while((s32[]{:T(128)}, f32[2048,512]{1,0:T(8,128)}, bf16[2048,4096]{1,0:T(8,128)(2,1)}, bf16[4096,512]{1,0:T(8,128)(2,1)}, ...), condition=%wide.region_1.2_spmd.clone, body=%wide.region_0.1_spmd.clone.sunk | while | flops 2151677952 | bytes 13633172 | solution.py:66
  416.9 6.8 %select_add_fusion.2 = f32[2048,512]{1,0:T(8,128)} fusion(f32[2048,512]{1,0:T(8,128)} %get-tuple-element.142, bf16[2048,4096]{1,0:T(8,128)(2,1)} %get-tuple-element.151, s32[]{:T(128)S(6)} %select_n.62, pred[]{:T(512)S(6)} %compare.9, bf16[4096,512]{1,0:T(8,128)(2,1)} %get-tuple-element.152), kind=kOutput, calls=%fused_computation.clone.1 | convolution fusion | flops 2151677952 | bytes 13633024 | tf_op jit(solution)/shard_map/while/body/eval_jaxpr/dot_general | solution.py:63
  423.8 8.1 %select_add_fusion.2 = f32[2048,512]{1,0:T(8,128)} fusion(f32[2048,512]{1,0:T(8,128)} %get-tuple-element.142, bf16[2048,4096]{1,0:T(8,128)(2,1)} %get-tuple-element.151, s32[]{:T(128)S(6)} %select_n.62, pred[]{:T(512)S(6)} %compare.9, bf16[4096,512]{1,0:T(8,128)(2,1)} %get-tuple-element.152), kind=kOutput, calls=%fused_computation.clone.1 | convolution fusion | flops 2151677952 | bytes 13633024 | tf_op jit(solution)/shard_map/while/body/eval_jaxpr/dot_general | solution.py:63
  431.9 8.1 %select_add_fusion.2 = f32[2048,512]{1,0:T(8,128)} fusion(f32[2048,512]{1,0:T(8,128)} %get-tuple-element.142, bf16[2048,4096]{1,0:T(8,128)(2,1)} %get-tuple-element.151, s32[]{:T(128)S(6)} %select_n.62, pred[]{:T(512)S(6)} %compare.9, bf16[4096,512]{1,0:T(8,128)(2,1)} %get-tuple-element.152), kind=kOutput, calls=%fused_computation.clone.1 | convolution fusion | flops 2151677952 | bytes 13633024 | tf_op jit(solution)/shard_map/while/body/eval_jaxpr/dot_general | solution.py:63
  440.0 8.1 %select_add_fusion.2 = f32[2048,512]{1,0:T(8,128)} fusion(f32[2048,512]{1,0:T(8,128)} %get-tuple-element.142, bf16[2048,4096]{1,0:T(8,128)(2,1)} %get-tuple-element.151, s32[]{:T(128)S(6)} %select_n.62, pred[]{:T(512)S(6)} %compare.9, bf16[4096,512]{1,0:T(8,128)(2,1)} %get-tuple-element.152), kind=kOutput, calls=%fused_computation.clone.1 | convolution fusion | flops 2151677952 | bytes 13633024 | tf_op jit(solution)/shard_map/while/body/eval_jaxpr/dot_general | solution.py:63
  448.1 4.2 fusion.18
  (2 shorter events, 0.0 us)
Async XLA Ops:
  6.5 6.9 %copy-start = (bf16[2048]{0:T(1024)(128)(2,1)S(1)}, bf16[2048]{0:T(1024)(128)(2,1)}, u32[]{:S(2)}) copy-start(bf16[2048]{0:T(1024)(128)(2,1)} %param.8) | copy-start | bytes 12292
  6.5 252.4 %all-gather.5.cloned.1.call-start = ((), (), s32[]{:S(2)}) async-start(), calls=%async_computation.2 | async-start | bytes 4718592 | tf_op jit(solution)/shard_map/all_gather | solution.py:54
  9.3 94.8 %collective-permute-start = (bf16[2048,512]{1,0:T(8,128)(2,1)S(1)}, bf16[2048,512]{1,0:T(8,128)(2,1)}, u32[]{:S(2)}, u32[]{:S(2)}) collective-permute-start(bf16[2048,512]{1,0:T(8,128)(2,1)S(1)} %multiply_convert_fusion), channel_id=1, source_target_pairs={{0,16},{16,0},{4,20},{20,4},{8,24},{24,8},{12,28},{28,12},{1,17},{... | collective-permute-start | bytes 6291464 | tf_op jit(solution)/shard_map/ppermute | solution.py:19
  107.1 47.0 %collective-permute-start.1 = (bf16[2048,512]{1,0:T(8,128)(2,1)S(1)}, bf16[2048,512]{1,0:T(8,128)(2,1)}, u32[]{:S(2)}, u32[]{:S(2)}) collective-permute-start(bf16[2048,512]{1,0:T(8,128)(2,1)S(1)} %fusion.12), channel_id=1, source_target_pairs={{0,8},{8,0},{4,12},{12,4},{16,24},{24,16},{20,28},{28,20},{1,9},{9... | collective-permute-start | bytes 6291464 | tf_op jit(solution)/shard_map/ppermute | solution.py:19
  212.7 204.2 %all-gather.3.cloned.1.call-start = ((), (), s32[]{:S(2)}) async-start(), calls=%async_computation.1 | async-start | bytes 20971520 | tf_op jit(solution)/shard_map/all_gather | solution.py:57
Sparse Core Ops, SparseCore 0:
  212.8 46.0 all-gather.4
  260.8 156.1 all-gather.2
where the time goes:
time: 459 us
  waiting for transfers between devices  335 us (73%)
  blocking collectives  54.4 us (12%)
  matrix products  31.1 us (7%)
  between operations  13.4 us (3%)
  other arithmetic  12.7 us (3%)
  local copies, waits for them, and re-layouts  7.97 us (2%)
  starting transfers between devices  4.83 us (1%)
    all_gather x1, waiting for transfers between devices, per_device(): shard_piece = lax.all_gather(panel_lower, 'col', axis=1, tiled=True)  152 us
    ppermute x2, waiting for transfers between devices, from_partner(): return lax.ppermute(block, axis, route)  137 us
    all_to_all x1, blocking collectives, per_device(): lax.all_to_all(transformed.reshape(row_count // groups, groups, col_width...  54.4 us
    all_gather x1, waiting for transfers between devices, per_device(): lax.all_gather(top_local, 'row', axis=1, tiled=True)  45.5 us
    dot_general x4, matrix products, one_block(): product = jnp.dot(panel_part, rows_used, preferred_element_type=jnp.float32)  31.1 us
  transfers between devices with their start and end apart: 4, of which 4 were waited for; matrix products, arithmetic and copies ran while one was open for 1% of the time, Pallas kernels for 0%

commit v1 on v0

v1 whole, which is shorter than its diff:
```python
import functools

import jax
import jax.numpy as jnp
from jax import lax
from jax.experimental import pallas as pl
from jax.experimental.pallas import tpu as pltpu
from jax.sharding import PartitionSpec as P

inv_root = 0.7071067811865476
F32, BF16 = jnp.float32, jnp.bfloat16


def column_of(row, size):
    a = lax.broadcasted_iota(jnp.int32, (size, size), 0)
    b = lax.broadcasted_iota(jnp.int32, (size, size), 1)
    return jnp.sum(jnp.where(a == b, row, 0.0), axis=1, keepdims=True)


def order_matrix(chunk, groups, natural_axis):
    per = chunk // groups
    natural = lax.broadcasted_iota(jnp.int32, (chunk, chunk), natural_axis)
    grouped = lax.broadcasted_iota(jnp.int32, (chunk, chunk), 1 - natural_axis)
    return jnp.where(natural == (grouped % per) * groups + grouped // per, 1.0, 0.0).astype(BF16)


def kernel(groups, cols, slab, s1, s2, panel, out, send, held, s2buf, tops, tops_nat, total, gath,
           own_sem, a2a_send, a2a_recv, s2_send, s2_recv, top_send, top_recv, fwd_send,
           pan_send, pan_recv):
    me, mc = lax.axis_index("row"), lax.axis_index("col")
    rows, width = slab.shape
    block = panel.shape[1]
    per_source = rows // groups
    top = cols * block // groups
    half = rows // 2
    chunk = max(256, 16 * groups)
    per = chunk // groups
    sibling = me + 1 - 2 * (me % 2)
    pairs = cols == 4
    col_x = mc + 1 - 2 * (mc % 2)
    col_y = mc + 2 - 4 * (mc // 2)

    def remote(src, dst, ssem, rsem, row=None, col=None):
        return pltpu.make_async_remote_copy(
            src_ref=src, dst_ref=dst, send_sem=ssem, recv_sem=rsem,
            device_id=(me if row is None else row, mc if col is None else col),
            device_id_type=pl.DeviceIdType.MESH)

    barrier = pltpu.get_barrier_semaphore()
    col_peers = [col_x, col_y] if pairs else [(mc + d) % cols for d in range(1, cols)]
    for d in range(1, groups):
        pl.semaphore_signal(barrier, inc=1, device_id=((me + d) % groups, mc),
                            device_id_type=pl.DeviceIdType.MESH)
    for peer in col_peers:
        pl.semaphore_signal(barrier, inc=1, device_id=(me, peer),
                            device_id_type=pl.DeviceIdType.MESH)
    own_panel = pltpu.make_async_copy(panel, gath.at[mc], own_sem.at[0])
    own_panel.start()
    pl.semaphore_wait(barrier, groups - 1 + len(col_peers))

    low, high = pl.ds(0, half), pl.ds(half, half)

    def panel_copy(n, part, peer, origin, src=None):
        source = panel.at[part] if src is None else src
        return remote(source, gath.at[origin, part], pan_send.at[n], pan_recv.at[n], col=peer)

    if pairs:
        panel_sends = [panel_copy(0, low, col_x, mc), panel_copy(1, high, col_y, mc),
                       panel_copy(2, high, col_x, mc), panel_copy(3, low, col_y, mc)]
    else:
        whole = pl.ds(0, rows)
        panel_sends = [panel_copy(d - 1, whole, (mc + d) % cols, mc) for d in range(1, cols)]
    for copy in panel_sends:
        copy.start()

    to_grouped = order_matrix(chunk, groups, 1)

    def scale_step(k, carry):
        scale = column_of(s1[pl.ds(k, 1), :], chunk)
        first = (scale * slab[pl.ds(k * chunk, chunk), :].astype(F32)).astype(BF16)
        moved = jnp.dot(to_grouped, first, preferred_element_type=F32).astype(BF16)
        for e in range(groups):
            send[e, pl.ds(k * per, per), :] = moved[e * per:(e + 1) * per]
        return carry

    lax.fori_loop(0, rows // chunk, scale_step, 0)
    place = pl.ds(me * per_source, per_source)
    exchange = []
    for d in range(1, groups):
        peer = (me + d) % groups
        exchange.append(remote(send.at[peer], held.at[place], a2a_send.at[d], a2a_recv.at[d],
                               row=peer))
        exchange.append(remote(s2, s2buf.at[me], s2_send.at[d], s2_recv.at[d], row=peer))
    for copy in exchange:
        copy.start()
    own_rows = pltpu.make_async_copy(send.at[me], held.at[place], own_sem.at[1])
    own_rows.start()
    own_scale = pltpu.make_async_copy(s2, s2buf.at[me], own_sem.at[2])
    own_scale.start()
    own_rows.wait()
    own_scale.wait()
    for d in range(1, groups):
        source = (me + groups - d) % groups
        remote(send.at[0], held.at[pl.ds(source * per_source, per_source)], a2a_send.at[d],
               a2a_recv.at[d], row=source).wait_recv()
        remote(s2, s2buf.at[source], s2_send.at[d], s2_recv.at[d], row=source).wait_recv()

    quarter = groups // 4

    def butterfly(u, carry):
        at = [pl.ds((u + n * quarter) * per_source, per_source) for n in range(4)]
        scale = [column_of(s2buf[u + n * quarter, pl.ds(me, 1), :], per_source) for n in range(4)]
        a = [held[at[n], :].astype(F32) for n in range(4)]
        one = [(a[0] + a[2]) * inv_root, (a[1] + a[3]) * inv_root,
               (a[0] - a[2]) * inv_root, (a[1] - a[3]) * inv_root]
        b = [(scale[n] * one[n]).astype(BF16).astype(F32) for n in range(4)]
        held[at[0], :] = ((b[0] + b[1]) * inv_root).astype(BF16)
        held[at[1], :] = ((b[0] - b[1]) * inv_root).astype(BF16)
        held[at[2], :] = ((b[2] + b[3]) * inv_root).astype(BF16)
        held[at[3], :] = ((b[2] - b[3]) * inv_root).astype(BF16)
        return carry

    lax.fori_loop(0, quarter, butterfly, 0)

    mine = held.at[pl.ds(0, top)]
    top_copies = []
    for d in range(2, groups, 2):
        top_copies.append(remote(mine, tops.at[me], top_send.at[d], top_recv.at[d],
                                 row=(me + d) % groups))
    top_copies.append(remote(mine, tops.at[me], top_send.at[0], top_recv.at[0], row=sibling))
    for copy in top_copies:
        copy.start()
    own_top = pltpu.make_async_copy(mine, tops.at[me], own_sem.at[3])
    own_top.start()

    if pairs:
        col_d = 3 - mc
        panel_sends[0].wait_recv()
        ahead = panel_copy(4, low, col_y, col_x, gath.at[col_x, low])
        ahead.start()
        panel_sends[1].wait_recv()
        across = panel_copy(5, high, col_x, col_y, gath.at[col_y, high])
        across.start()
        panel_sends += [ahead, across]

    forwards = []
    for d in range(2, groups, 2):
        source = (me + groups - d) % groups
        remote(mine, tops.at[source], top_send.at[d], top_recv.at[d], row=source).wait_recv()
        forward = remote(tops.at[source], tops.at[source], fwd_send.at[d], top_recv.at[d + 1],
                         row=sibling)
        forward.start()
        forwards.append(forward)
    own_top.wait()
    remote(mine, tops.at[sibling], top_send.at[0], top_recv.at[0], row=sibling).wait_recv()
    for d in range(2, groups, 2):
        source = (sibling + groups - d) % groups
        remote(tops.at[source], tops.at[source], fwd_send.at[d], top_recv.at[d + 1],
               row=sibling).wait_recv()

    to_natural = order_matrix(chunk, groups, 0)

    def natural_step(k, carry):
        pieces = [tops[e, pl.ds(k * per, per), :] for e in range(groups)]
        rows_now = jnp.dot(to_natural, jnp.concatenate(pieces, axis=0), preferred_element_type=F32)
        tops_nat[pl.ds(k * chunk, chunk), :] = rows_now.astype(BF16)
        return carry

    lax.fori_loop(0, cols * block // chunk, natural_step, 0)

    tile = 256

    def term(b, at):
        product = jnp.dot(gath[b, at, :], tops_nat[pl.ds(b * block, block), :],
                          preferred_element_type=F32)
        return product.astype(BF16).astype(F32)

    own_panel.wait()
    if pairs:
        panel_sends[2].wait_recv()
        panel_sends[3].wait_recv()

        def near_step(t, carry):
            at = pl.ds(t * tile, tile)
            total[at, :] = held[at, :].astype(F32) - (term(mc, at) + term(col_x, at) + term(col_y, at))
            return carry

        def far_step(t, carry):
            at = pl.ds(t * tile, tile)
            out[at, :] = (total[at, :] - term(col_d, at)).astype(BF16)
            return carry

        lax.fori_loop(0, rows // tile, near_step, 0)
        panel_copy(4, low, col_y, col_d, gath.at[col_d, low]).wait_recv()
        lax.fori_loop(0, half // tile, far_step, 0)
        panel_copy(5, high, col_x, col_d, gath.at[col_d, high]).wait_recv()
        lax.fori_loop(half // tile, rows // tile, far_step, 0)
    else:
        for copy in panel_sends:
            copy.wait_recv()

        def all_step(t, carry):
            at = pl.ds(t * tile, tile)

            def add(b, run):
                return run + term(b, at)

            update = lax.fori_loop(0, cols, add, jnp.zeros((tile, width), F32))
            out[at, :] = (held[at, :].astype(F32) - update).astype(BF16)
            return carry

        lax.fori_loop(0, rows // tile, all_step, 0)

    for copy in exchange + top_copies + forwards + panel_sends:
        copy.wait_send()


def per_device(slab_block, scale_first, scale_second, panel_lower):
    rows, width = slab_block.shape
    block = panel_lower.shape[1]
    groups, cols = lax.axis_size("row"), lax.axis_size("col")
    per_source = rows // groups
    top = cols * block // groups
    chunk = max(256, 16 * groups)
    s1 = scale_first.astype(F32).reshape(rows // chunk, chunk)
    s2 = scale_second.astype(F32).reshape(per_source, groups).T
    vmem = pl.BlockSpec(memory_space=pltpu.VMEM)
    dma = pltpu.SemaphoreType.DMA
    return pl.pallas_call(
        functools.partial(kernel, groups, cols),
        out_shape=jax.ShapeDtypeStruct((rows, width), BF16),
        in_specs=[vmem, vmem, vmem, pl.BlockSpec(memory_space=pl.ANY)],
        out_specs=vmem,
        scratch_shapes=[
            pltpu.VMEM((groups, per_source, width), BF16),
            pltpu.VMEM((rows, width), BF16),
            pltpu.VMEM((groups, groups, per_source), F32),
            pltpu.VMEM((groups, top, width), BF16),
            pltpu.VMEM((cols * block, width), BF16),
            pltpu.VMEM((rows, width), F32),
            pltpu.VMEM((cols, rows, block), BF16),
            dma((4,)),
            dma((groups,)), dma((groups,)), dma((groups,)), dma((groups,)),
            dma((groups,)), dma((groups,)), dma((groups,)),
            dma((max(6, cols),)), dma((max(6, cols),)),
        ],
        compiler_params=pltpu.CompilerParams(
            collective_id=0, has_side_effects=True, vmem_limit_bytes=56 * 2**20),
        cost_estimate=pl.CostEstimate(
            flops=2 * rows * cols * block * width,
            bytes_accessed=2 * (rows * width * 2 + rows * block), transcendentals=0),
    )(slab_block, s1, s2, panel_lower)


def solution(mesh):
    placed = (P("row", "col"), P("row"), P("row"), P("row", "col"))
    return jax.shard_map(
        per_device, mesh=mesh, in_specs=placed, out_specs=P("row", "col"), check_vma=False
    )
```

time: 459 us -> 156 us (0.34)
  waiting for transfers between devices: 335 us -> 0 us
  Pallas kernels: 0 us -> 150 us
  blocking collectives: 54.4 us -> 0 us
  matrix products: 31.1 us -> 0 us
  between operations: 13.4 us -> 0.02 us
  other arithmetic: 12.7 us -> 0 us
  starting transfers between devices: 4.83 us -> 0 us
    all_gather x2 -> x0, waiting for transfers between devices: 197 us -> none  [the longest x1 152 us: per_device(): shard_piece = lax.all_gather(panel_lower, 'col', axis=1, tiled=True)]
    pallas_call x0 -> x1, Pallas kernels: none -> 150 us  [per_device(): pl.pallas_call(functools.partial(kernel, groups, cols), out_shape=jax.Sha...]
    ppermute x2 -> x0, waiting for transfers between devices: 137 us -> none  [from_partner(): return lax.ppermute(block, axis, route)]
    all_to_all x1 -> x0, blocking collectives: 54.4 us -> none  [per_device(): lax.all_to_all(transformed.reshape(row_count // groups, groups, col_width...]
    dot_general x4 -> x0, matrix products: 31.1 us -> none  [one_block(): product = jnp.dot(panel_part, rows_used, preferred_element_type=jnp.float32)]
    convert_element_type x5 -> x0, other arithmetic: 10 us -> none  [the longest x1 4.22 us: per_device(): return (stored.astype(jnp.float32) - update_sum).astype(jnp.bfloat16)]
    all_gather x1 -> x0, local copies, waits for them, and re-layouts: 6.47 us -> none  [per_device(): lax.all_gather(top_local, 'row', axis=1, tiled=True)]
    ppermute x2 -> x0, starting transfers between devices: 4.78 us -> none  [from_partner(): return lax.ppermute(block, axis, route)]
  transfers between devices with their start and end apart: 4 -> 0, of which waited for: 4 -> 0; matrix products, arithmetic and copies ran while one was open for 1% -> 0% of each run, Pallas kernels for 0% -> 0%
where the time goes in v1:
time: 156 us
  Pallas kernels  150 us (96%)
  local copies, waits for them, and re-layouts  5.78 us (4%)
    pallas_call x1, Pallas kernels, per_device(): pl.pallas_call(functools.partial(kernel, groups, cols), out_shape=jax.Sha...  150 us

profile of v1, /device:TPU:0, one launch (start us, length us, event | category | flops | bytes accessed | tf_op | source)
XLA Modules:
  0.0 155.6 jit_solution(15408296682595381945)
XLA Ops:
  0.0 1.3 reshape.13.s1
  1.3 0.8 reshape.14
  2.1 0.7 copy.5
  2.7 149.8 %shard_map.46 = bf16[2048,512]{1,0:T(8,128)(2,1)} custom-call(bf16[2048,512]{1,0:T(8,128)(2,1)} %slab.1, f32[8,256]{1,0:T(8,128)} %reshape.13.s1, f32[8,256]{1,0:T(8,128)} %bitcast.1, bf16[2048,1024]{1,0:T(8,128)(2,1)} %panel.1), custom_call_target="tpu_custom_call" | custom-call | flops 8589934592 | bytes 8388608 | tf_op jit(solution)/shard_map/pallas_call | solution.py:229
  152.5 3.0 %copy.7 = bf16[2048,512]{1,0:T(8,128)(2,1)} copy(bf16[2048,512]{1,0:T(8,128)(2,1)} %shard_map.46) | data formatting | bytes 4194304

commit v2 on v1

--- a/solution.py
+++ b/solution.py
@@ -215,6 +215,368 @@
         copy.wait_send()
 
 
+def paired_kernel(groups, parts, slab, scales, panel, out, send, held, s2buf, tops, tops_x, tops_y,
+                  own, near_x, near_y, part_out, part_in, total,
+                  own_sem, a2a_send, a2a_recv, s2_send, s2_recv, top_recv, chain_send, core_send,
+                  x_send, x_recv, y_send, y_recv, xc_send, yc_send, sum_send, sum_recv,
+                  pan_send, pan_recv):
+    me, mc = lax.axis_index("row"), lax.axis_index("col")
+    rows, _ = slab.shape
+    width = held.shape[2]
+    per_source = rows // groups
+    half = rows // 2
+    chunk = 256
+    per = chunk // groups
+    chips = groups // 2
+    z, core = me // 2, me % 2
+    y, x = mc // 2, mc % 2
+    sibling = me + 1 - 2 * core
+    col_x = mc + 1 - 2 * x
+    col_y = mc + 2 - 4 * y
+    block_rows = tops.shape[4]
+    lines = rows // chunk
+    s2 = scales.at[pl.ds(lines, lines)]
+
+    def remote(src, dst, ssem, rsem, row=None, col=None):
+        return pltpu.make_async_remote_copy(
+            src_ref=src, dst_ref=dst, send_sem=ssem, recv_sem=rsem,
+            device_id=(me if row is None else row, mc if col is None else col),
+            device_id_type=pl.DeviceIdType.MESH)
+
+    barrier = pltpu.get_barrier_semaphore()
+    for d in range(1, groups):
+        pl.semaphore_signal(barrier, inc=1, device_id=((me + d) % groups, mc),
+                            device_id_type=pl.DeviceIdType.MESH)
+    for peer in (col_x, col_y):
+        pl.semaphore_signal(barrier, inc=1, device_id=(me, peer),
+                            device_id_type=pl.DeviceIdType.MESH)
+    own_panel = pltpu.make_async_copy(panel, own, own_sem.at[0])
+    own_panel.start()
+    pl.semaphore_wait(barrier, groups + 1)
+
+    panel_x = remote(panel.at[pl.ds(0, half)], near_x, pan_send.at[0], pan_recv.at[0], col=col_x)
+    panel_y = remote(panel.at[pl.ds(half, half)], near_y, pan_send.at[1], pan_recv.at[1], col=col_y)
+    panel_x.start()
+    panel_y.start()
+
+    to_grouped = order_matrix(chunk, groups, 1)
+    place = pl.ds(me * per_source, per_source)
+
+    def scaled(q):
+        def step(k, carry):
+            scale = column_of(scales[pl.ds(k, 1), :], chunk)
+            lanes = slice(q * width, (q + 1) * width)
+            first = (scale * slab[pl.ds(k * chunk, chunk), lanes].astype(F32)).astype(BF16)
+            moved = jnp.dot(to_grouped, first, preferred_element_type=F32).astype(BF16)
+            for e in range(groups):
+                send[q, e, pl.ds(k * per, per), :] = moved[e * per:(e + 1) * per]
+            return carry
+
+        lax.fori_loop(0, rows // chunk, step, 0)
+
+    def exchange(q):
+        for d in range(1, groups):
+            peer = (me + d) % groups
+            copy = remote(send.at[q, peer], held.at[q, place], a2a_send.at[q, d],
+                          a2a_recv.at[q, d], row=peer)
+            copy.start()
+            sends.append(copy)
+
+    sends = []
+    for d in range(1, groups):
+        peer = (me + d) % groups
+        copy = remote(s2, s2buf.at[me], s2_send.at[d], s2_recv.at[d], row=peer)
+        copy.start()
+        sends.append(copy)
+    scaled(0)
+    exchange(0)
+    for q in range(1, parts):
+        scaled(q)
+    own_copies = [pltpu.make_async_copy(s2, s2buf.at[me], own_sem.at[1])]
+    for q in range(parts):
+        own_copies.append(pltpu.make_async_copy(send.at[q, me], held.at[q, place],
+                                                own_sem.at[2 + q]))
+    for copy in own_copies:
+        copy.start()
+
+    to_columns = order_matrix(chunk, groups, 0)
+
+    def regroup(ref):
+        def step(t, carry):
+            at = pl.ds(t * chunk, chunk)
+            for n in range(ref.shape[1] // chunk):
+                lanes = slice(n * chunk, (n + 1) * chunk)
+                ref[at, lanes] = jnp.dot(ref[at, lanes], to_columns,
+                                         preferred_element_type=F32).astype(BF16)
+            return carry
+
+        lax.fori_loop(0, ref.shape[0] // chunk, step, 0)
+
+    own_panel.wait()
+    regroup(own)
+    for copy in own_copies:
+        copy.wait()
+    for d in range(1, groups):
+        source = (me + groups - d) % groups
+        remote(s2, s2buf.at[source], s2_send.at[d], s2_recv.at[d], row=source).wait_recv()
+
+    quarter = groups // 4
+
+    def top_rows(q):
+        for d in range(1, groups):
+            source = (me + groups - d) % groups
+            remote(send.at[q, 0], held.at[q, pl.ds(source * per_source, per_source)],
+                   a2a_send.at[q, d], a2a_recv.at[q, d], row=source).wait_recv()
+
+        def step(u, carry):
+            a = [held[q, source_rows(u, n), :].astype(F32) for n in range(4)]
+            one = [(a[0] + a[2]) * inv_root, (a[1] + a[3]) * inv_root]
+            b = [(second_scale(u + n * quarter) * one[n]).astype(BF16).astype(F32)
+                 for n in range(2)]
+            upper = ((b[0] + b[1]) * inv_root).astype(BF16)
+            tops[q, me, u, 0] = upper[:block_rows]
+            tops[q, me, u, 1] = upper[block_rows:]
+            return carry
+
+        lax.fori_loop(0, quarter, step, 0)
+
+    def source_rows(u, n):
+        return pl.ds((u + n * quarter) * per_source, per_source)
+
+    def second_scale(source):
+        j = lax.broadcasted_iota(jnp.int32, (per, chunk), 0)
+        natural = lax.broadcasted_iota(jnp.int32, (per, chunk), 1)
+        here = natural == j * groups + me
+        return jnp.concatenate(
+            [jnp.sum(jnp.where(here, s2buf[source, k:k + 1, :], 0.0), axis=1, keepdims=True)
+             for k in range(lines)], axis=0)
+
+    def all_rows(q):
+        def step(u, carry):
+            at = [source_rows(u, n) for n in range(4)]
+            a = [held[q, at[n], :].astype(F32) for n in range(4)]
+            one = [(a[0] + a[2]) * inv_root, (a[1] + a[3]) * inv_root,
+                   (a[0] - a[2]) * inv_root, (a[1] - a[3]) * inv_root]
+            b = [(second_scale(u + n * quarter) * one[n]).astype(BF16).astype(F32)
+                 for n in range(4)]
+            held[q, at[0], :] = ((b[0] + b[1]) * inv_root).astype(BF16)
+            held[q, at[1], :] = ((b[0] - b[1]) * inv_root).astype(BF16)
+            held[q, at[2], :] = ((b[2] + b[3]) * inv_root).astype(BF16)
+            held[q, at[3], :] = ((b[2] - b[3]) * inv_root).astype(BF16)
+            return carry
+
+        lax.fori_loop(0, quarter, step, 0)
+
+    def chain(q, chip, way):
+        e = 2 * chip + core
+        to = (me + 2) % groups if way == 0 else (me + groups - 2) % groups
+        return remote(tops.at[q, e], tops.at[q, e], chain_send.at[q, way, chip],
+                      top_recv.at[q, e], row=to)
+
+    def to_core(q, e):
+        return remote(tops.at[q, e], tops.at[q, e], core_send.at[q, e], top_recv.at[q, e],
+                      row=sibling)
+
+    def to_x(q, e):
+        return remote(tops.at[q, e, :, 1 - x], tops_x.at[q, e], x_send.at[q, e], x_recv.at[q, e],
+                      col=col_x)
+
+    def to_y(q, e):
+        return remote(tops.at[q, e, 1 - y], tops_y.at[q, e], y_send.at[q, e], y_recv.at[q, e],
+                      col=col_y)
+
+    def x_core(q, e):
+        return remote(tops_x.at[q, e], tops_x.at[q, e], xc_send.at[q, e], x_recv.at[q, e],
+                      row=sibling)
+
+    def y_core(q, e):
+        return remote(tops_y.at[q, e], tops_y.at[q, e], yc_send.at[q, e], y_recv.at[q, e],
+                      row=sibling)
+
+    def spread(q, chip):
+        e = 2 * chip + core
+        to_x(q, e).start()
+        to_y(q, e).start()
+        to_core(q, e).start()
+
+    def begin(q):
+        @pl.when(z + 1 < chips)
+        def _():
+            chain(q, z, 0).start()
+
+        @pl.when(z > 0)
+        def _():
+            chain(q, z, 1).start()
+
+        spread(q, z)
+
+    def onward(q, k):
+        @pl.when(z >= k)
+        def _():
+            chain(q, z - k, 0).wait_recv()
+
+            @pl.when(z + 1 < chips)
+            def _():
+                chain(q, z - k, 0).start()
+
+            spread(q, z - k)
+
+        @pl.when(z + k < chips)
+        def _():
+            chain(q, z + k, 1).wait_recv()
+
+            @pl.when(z > 0)
+            def _():
+                chain(q, z + k, 1).start()
+
+            spread(q, z + k)
+
+    def collect(q):
+        for chip in range(chips):
+            e = 2 * chip + core
+            to_x(q, e).wait_recv()
+            x_core(q, e).start()
+            to_y(q, e).wait_recv()
+            y_core(q, e).start()
+        for chip in range(chips):
+            other = 2 * chip + 1 - core
+            to_core(q, other).wait_recv()
+            x_core(q, other).wait_recv()
+            y_core(q, other).wait_recv()
+
+    pieces = [(e, slice(n * per, (n + 1) * per))
+              for n in range(block_rows // per) for e in range(groups)]
+
+    def own_top(q, by, bx):
+        return jnp.concatenate([tops[q, e, by, bx, at, :] for e, at in pieces], axis=0)
+
+    def far_top(ref, q, b):
+        return jnp.concatenate([ref[q, e, b, at, :] for e, at in pieces], axis=0)
+
+    tile = 256
+    tiles = half // tile
+
+    def product(a, b):
+        return jnp.dot(a, b, preferred_element_type=F32)
+
+    def sum_copy(q, t, high):
+        at = pl.ds(t * tile + (half if high else 0), tile)
+        n = t + (tiles if high else 0)
+        return remote(part_out.at[q, at], part_in.at[q, at], sum_send.at[q, n], sum_recv.at[q, n],
+                      col=col_x if high else col_y)
+
+    def send_sums(q):
+        def step(t, carry):
+            at, upper = pl.ds(t * tile, tile), pl.ds(half + t * tile, tile)
+            part_out[q, at, :] = (product(own[at, :], far_top(tops_y, q, x)) +
+                                  product(near_x[at, :], far_top(tops_y, q, 1 - x))).astype(BF16)
+            sum_copy(q, t, False).start()
+            part_out[q, upper, :] = (product(own[upper, :], far_top(tops_x, q, y)) +
+                                     product(near_y[at, :], far_top(tops_x, q, 1 - y))
+                                     ).astype(BF16)
+            sum_copy(q, t, True).start()
+            return carry
+
+        lax.fori_loop(0, tiles, step, 0)
+
+    def own_sums(q):
+        def step(t, carry):
+            at, upper = pl.ds(t * tile, tile), pl.ds(half + t * tile, tile)
+            mine = own_top(q, y, x)
+            total[q, at, :] = held[q, at, :].astype(F32) - (
+                product(own[at, :], mine) + product(near_x[at, :], own_top(q, y, 1 - x)))
+            total[q, upper, :] = held[q, upper, :].astype(F32) - (
+                product(own[upper, :], mine) + product(near_y[at, :], own_top(q, 1 - y, x)))
+            return carry
+
+        lax.fori_loop(0, tiles, step, 0)
+
+    def finish(q):
+        lanes = slice(q * width, (q + 1) * width)
+
+        def step(t, carry):
+            for high in (False, True):
+                sum_copy(q, t, high).wait_recv()
+                at = pl.ds(t * tile + (half if high else 0), tile)
+                out[at, lanes] = (total[q, at, :] - part_in[q, at, :].astype(F32)).astype(BF16)
+            return carry
+
+        lax.fori_loop(0, tiles, step, 0)
+
+    top_rows(0)
+    begin(0)
+    exchange(1)
+    all_rows(0)
+    onward(0, 1)
+    panel_x.wait_recv()
+    panel_y.wait_recv()
+    regroup(near_x)
+    regroup(near_y)
+    onward(0, 2)
+    top_rows(1)
+    begin(1)
+    all_rows(1)
+    onward(0, 3)
+    onward(1, 1)
+    collect(0)
+    onward(1, 2)
+    send_sums(0)
+    onward(1, 3)
+    own_sums(0)
+    collect(1)
+    send_sums(1)
+    own_sums(1)
+    finish(0)
+    finish(1)
+
+    for copy in sends + [panel_x, panel_y]:
+        copy.wait_send()
+    for q in range(parts):
+        for chip in range(chips):
+            @pl.when((z + 1 < chips) & (chip <= z))
+            def _():
+                chain(q, chip, 0).wait_send()
+
+            @pl.when((z > 0) & (chip >= z))
+            def _():
+                chain(q, chip, 1).wait_send()
+
+            e = 2 * chip + core
+            for copy in (to_x(q, e), to_y(q, e), to_core(q, e), x_core(q, e), y_core(q, e)):
+                copy.wait_send()
+
+        def done(t, carry):
+            sum_copy(q, t, False).wait_send()
+            sum_copy(q, t, True).wait_send()
+            return carry
+
+        lax.fori_loop(0, tiles, done, 0)
+
+
+def paired_scratch(groups, parts, rows, block, width):
+    dma = pltpu.SemaphoreType.DMA
+    piece, upper = width // parts, block // groups
+    pair = dma((parts, groups))
+    return [
+        pltpu.VMEM((parts, groups, rows // groups, piece), BF16),
+        pltpu.VMEM((parts, rows, piece), BF16),
+        pltpu.VMEM((groups, rows // 256, 256), F32),
+        pltpu.VMEM((parts, groups, 2, 2, upper, piece), BF16),
+        pltpu.VMEM((parts, groups, 2, upper, piece), BF16),
+        pltpu.VMEM((parts, groups, 2, upper, piece), BF16),
+        pltpu.VMEM((rows, block), BF16),
+        pltpu.VMEM((rows // 2, block), BF16),
+        pltpu.VMEM((rows // 2, block), BF16),
+        pltpu.VMEM((parts, rows, piece), BF16),
+        pltpu.VMEM((parts, rows, piece), BF16),
+        pltpu.VMEM((parts, rows, piece), F32),
+        dma((2 + parts,)), pair, pair, dma((groups,)), dma((groups,)), pair,
+        dma((parts, 2, groups // 2)), pair,
+        pair, pair, pair, pair, pair, pair,
+        dma((parts, rows // 256)), dma((parts, rows // 256)), dma((2,)), dma((2,)),
+    ]
+
+
 def per_device(slab_block, scale_first, scale_second, panel_lower):
     rows, width = slab_block.shape
     block = panel_lower.shape[1]
@@ -222,16 +584,19 @@
     per_source = rows // groups
     top = cols * block // groups
     chunk = max(256, 16 * groups)
-    s1 = scale_first.astype(F32).reshape(rows // chunk, chunk)
-    s2 = scale_second.astype(F32).reshape(per_source, groups).T
     vmem = pl.BlockSpec(memory_space=pltpu.VMEM)
     dma = pltpu.SemaphoreType.DMA
-    return pl.pallas_call(
-        functools.partial(kernel, groups, cols),
-        out_shape=jax.ShapeDtypeStruct((rows, width), BF16),
-        in_specs=[vmem, vmem, vmem, pl.BlockSpec(memory_space=pl.ANY)],
-        out_specs=vmem,
-        scratch_shapes=[
+    if groups == 8 and cols == 4 and rows == 2 * block and width % 256 == 0:
+        parts = 2
+        run = functools.partial(paired_kernel, groups, parts)
+        both = jnp.concatenate([scale_first, scale_second]).astype(F32)
+        scales = [both.reshape(2 * rows // chunk, chunk)]
+        scratch = paired_scratch(groups, parts, rows, block, width)
+    else:
+        run = functools.partial(kernel, groups, cols)
+        scales = [scale_first.astype(F32).reshape(rows // chunk, chunk),
+                  scale_second.astype(F32).reshape(per_source, groups).T]
+        scratch = [
             pltpu.VMEM((groups, per_source, width), BF16),
             pltpu.VMEM((rows, width), BF16),
             pltpu.VMEM((groups, groups, per_source), F32),
@@ -243,13 +608,19 @@
             dma((groups,)), dma((groups,)), dma((groups,)), dma((groups,)),
             dma((groups,)), dma((groups,)), dma((groups,)),
             dma((max(6, cols),)), dma((max(6, cols),)),
-        ],
+        ]
+    return pl.pallas_call(
+        run,
+        out_shape=jax.ShapeDtypeStruct((rows, width), BF16),
+        in_specs=[vmem] * (1 + len(scales)) + [pl.BlockSpec(memory_space=pl.ANY)],
+        out_specs=vmem,
+        scratch_shapes=scratch,
         compiler_params=pltpu.CompilerParams(
             collective_id=0, has_side_effects=True, vmem_limit_bytes=56 * 2**20),
         cost_estimate=pl.CostEstimate(
             flops=2 * rows * cols * block * width,
             bytes_accessed=2 * (rows * width * 2 + rows * block), transcendentals=0),
-    )(slab_block, s1, s2, panel_lower)
+    )(slab_block, *scales, panel_lower)
 
 
 def solution(mesh):

time: 156 us -> 128 us (0.82)
  Pallas kernels: 150 us -> 122 us
    pallas_call x1, Pallas kernels: 150 us -> 122 us  [per_device(): pl.pallas_call(run, out_shape=jax.ShapeDtypeStruct((rows, width), BF16),...]
where the time goes in v2:
time: 128 us; the launch traced here: 127 us
  Pallas kernels  122 us (95%)
  local copies, waits for them, and re-layouts  4.43 us (3%)
    pallas_call x1, Pallas kernels, per_device(): pl.pallas_call(run, out_shape=jax.ShapeDtypeStruct((rows, width), BF16),...  122 us
    unnamed x1, local copies, waits for them, and re-layouts  3.05 us

profile of v2, /device:TPU:0, one launch (start us, length us, event | category | flops | bytes accessed | tf_op | source)
XLA Modules:
  0.0 127.5 jit_solution(16846159076153104027)
XLA Ops:
  0.0 0.7 concatenate.8
  0.7 0.7 concatenate.9
  1.4 0.6 maximum_convert_fusion.scales
  2.0 122.4 %shard_map.46 = bf16[2048,512]{1,0:T(8,128)(2,1)} custom-call(bf16[2048,512]{1,0:T(8,128)(2,1)} %slab.1, f32[16,256]{1,0:T(8,128)} %maximum_convert_fusion.scales, bf16[2048,1024]{1,0:T(8,128)(2,1)} %panel.1), custom_call_target="tpu_custom_call" | custom-call | flops 8589934592 | bytes 8388608 | tf_op jit(solution)/shard_map/pallas_call | solution.py:612
  124.4 3.0 %copy.6 = bf16[2048,512]{1,0:T(8,128)(2,1)} copy(bf16[2048,512]{1,0:T(8,128)(2,1)} %shard_map.46) | data formatting | bytes 4194304

commit v3 on v2

--- a/solution.py
+++ b/solution.py
@@ -505,9 +505,9 @@
 
     top_rows(0)
     begin(0)
-    exchange(1)
     all_rows(0)
     onward(0, 1)
+    exchange(1)
     panel_x.wait_recv()
     panel_y.wait_recv()
     regroup(near_x)
@@ -522,11 +522,11 @@
     onward(1, 2)
     send_sums(0)
     onward(1, 3)
-    own_sums(0)
     collect(1)
     send_sums(1)
+    own_sums(0)
+    finish(0)
     own_sums(1)
-    finish(0)
     finish(1)
 
     for copy in sends + [panel_x, panel_y]:

time: 128 us -> 125 us (0.977)
  Pallas kernels: 122 us -> 120 us
    pallas_call x1, Pallas kernels: 122 us -> 120 us  [per_device(): pl.pallas_call(run, out_shape=jax.ShapeDtypeStruct((rows, width), BF16),...]
where the time goes in v3:
time: 125 us
  Pallas kernels  120 us (96%)
  local copies, waits for them, and re-layouts  4.43 us (4%)
    pallas_call x1, Pallas kernels, per_device(): pl.pallas_call(run, out_shape=jax.ShapeDtypeStruct((rows, width), BF16),...  120 us
    unnamed x1, local copies, waits for them, and re-layouts  3.05 us

profile of v3, /device:TPU:0, one launch (start us, length us, event | category | flops | bytes accessed | tf_op | source)
XLA Modules:
  0.0 125.1 jit_solution(16952126266964618583)
XLA Ops:
  0.0 0.7 concatenate.8
  0.7 0.7 concatenate.9
  1.4 0.6 maximum_convert_fusion.scales
  2.0 120.0 %shard_map.46 = bf16[2048,512]{1,0:T(8,128)(2,1)} custom-call(bf16[2048,512]{1,0:T(8,128)(2,1)} %slab.1, f32[16,256]{1,0:T(8,128)} %maximum_convert_fusion.scales, bf16[2048,1024]{1,0:T(8,128)(2,1)} %panel.1), custom_call_target="tpu_custom_call" | custom-call | flops 8589934592 | bytes 8388608 | tf_op jit(solution)/shard_map/pallas_call | solution.py:612
  122.1 3.0 %copy.6 = bf16[2048,512]{1,0:T(8,128)(2,1)} copy(bf16[2048,512]{1,0:T(8,128)(2,1)} %shard_map.46) | data formatting | bytes 4194304
